TPU v7x, 512 devices: a whole 4x8x8 slice. The times are simulated.
512 devices in a mesh: lat: 2 (over core), lon: 8 (over y), mem: 32 (over z, x).
Axes of the slice: x: 4, y: 8, z: 8, core: 2. Of those that a mesh axis runs over, the one named last changes fastest.
Arguments:
- alpha: float32 [128, 64, 16, 1024], P(None, 'mem', 'lat', 'lon'), may hold values from -4 to 7
- perturb: bfloat16 [128, 64, 16, 1024], P(None, 'mem', 'lat', 'lon'), may hold values from -6 to 6
- smooth_gain: float32 [16, 1024], replicated, may hold values from 0.25 to 1
- bands: int32 [128], replicated, may hold values from 1 to 8, as said below
- steps: int32 [128], replicated, may hold values from 1 to 24, as said below
Outputs:
- increment: float32 [128, 16, 1024], P('mem', 'lat', 'lon')
Inputs may be any that keep to these rules, and one draw needn't show every extreme that they name: `bands`: 8 is reached at some level. `steps`: 24 is reached at some level.
All inputs are finite; a program needn't handle non-finite values.
Results may differ from a plain program's by a relative error of at most 0.0003.
Values may be sent and summed in bfloat16 or wider, within the bound.
A program may use at most 64 MiB of HBM per device.

v0:
```python
import math

import jax
import jax.numpy as jnp
from jax import lax
from jax.sharding import PartitionSpec as P


def band_weights(bands, levels):
    level_rows = jnp.arange(levels, dtype=jnp.int32)
    distance = jnp.abs(level_rows[:, None] - level_rows[None, :]).astype(jnp.float32)
    band_width = bands.astype(jnp.float32)[:, None]
    raw_weights = jnp.where(distance <= band_width, 1.0 - distance / (band_width + 1.0), 0.0)
    return raw_weights / jnp.sum(raw_weights, axis=1, keepdims=True)


def diffuse_all(values_in, coefficient, counts):
    limit = jnp.max(counts)
    active_counts = counts[:, None, None, None]

    def one_step(step_index, state_now):
        padded = jnp.pad(state_now, ((0, 0), (0, 0), (1, 1), (1, 1)), mode="edge")
        beside_all = (
            padded[:, :, 2:, 1:-1]
            + padded[:, :, :-2, 1:-1]
            + padded[:, :, 1:-1, 2:]
            + padded[:, :, 1:-1, :-2]
        )
        updated = state_now + coefficient * (beside_all - 4.0 * state_now)
        return jnp.where(step_index < active_counts, updated, state_now)

    return lax.fori_loop(0, limit, one_step, values_in)


def body(alpha, perturb, smooth_gain, bands, steps):
    lat_count = lax.axis_size("lat")
    lon_count = lax.axis_size("lon")
    levels = alpha.shape[0]
    members_here = alpha.shape[1]
    weights = band_weights(bands, levels)
    vertical = jnp.einsum(
        "lk,kmc->lmc",
        weights,
        alpha.reshape(levels, members_here, -1),
        precision=lax.Precision.HIGHEST,
        preferred_element_type=jnp.float32,
    ).reshape(alpha.shape)
    coefficient = 0.24 * smooth_gain
    member_scale = 1.0 / math.sqrt(members_here * lax.axis_size("mem"))
    owners = lat_count * lon_count
    per_owner = levels // owners
    source = jnp.arange(levels, dtype=jnp.int32)
    slabs = lax.all_to_all(
        lax.all_to_all(vertical, "lat", split_axis=0, concat_axis=2, tiled=True),
        "lon",
        split_axis=0,
        concat_axis=3,
        tiled=True,
    )
    owner_index = lax.axis_index("lat") * lon_count + lax.axis_index("lon")
    own_levels = lax.dynamic_slice_in_dim(source, owner_index * per_owner, per_owner)
    own_counts = jnp.take(steps, own_levels)
    smoothed = diffuse_all(slabs, coefficient, own_counts)
    returned = lax.all_to_all(smoothed, "lon", split_axis=3, concat_axis=0, tiled=True)
    returned = lax.all_to_all(returned, "lat", split_axis=2, concat_axis=0, tiled=True)
    products = perturb.astype(jnp.float32) * returned
    partial_value = jnp.sum(products, axis=1) * member_scale
    return lax.psum_scatter(partial_value, "mem", scatter_dimension=0, tiled=True)


def solution(mesh):
    placed = (P(None, "mem", "lat", "lon"), P(None, "mem", "lat", "lon"), P(), P(), P())
    return jax.shard_map(
        body, mesh=mesh, in_specs=placed, out_specs=P("mem", "lat", "lon"), check_vma=False
    )
```

profile of v0, /device:TPU:1, one launch (start us, length us, event | category | flops | bytes accessed | tf_op | source)
XLA Modules:
  0.0 404.9 jit_solution(932436303850699349)
XLA Ops:
  6.5 0.7 broadcast_add_fusion
  7.2 0.7 convert_element_type.13
  7.9 1.7 reshape.26
  9.6 0.5 copy.23
  10.1 0.2 fusion.17
  10.3 1.1 fusion.14
  11.4 0.6 copy.24
  12.0 11.1 %all_to_all.72 = f32[128,2,8,128]{3,2,1,0:T(8,128)S(1)} all-to-all(f32[128,2,8,128]{3,2,1,0:T(8,128)S(1)} %copy.24), channel_id=1, replica_groups=mesh['lat'=2,'lon'=8,'mem'=32] {'lat'}, dimensions={0} | all-to-all | bytes 2097152 | tf_op jit(solution)/shard_map/all_to_all | solution.py:54
  23.1 1.1 copy.42
  24.2 3.6 all-to-all-start.1
  28.0 0.6 gather_fusion
  28.6 0.8 fusion.25
  29.4 27.6 %all-to-all-done.1 = f32[64,2,16,128]{3,2,1,0:T(8,128)S(1)} async-done(((f32[64,2,16,128]{3,2,1,0:T(8,128)}), f32[64,2,16,128]{3,2,1,0:T(8,128)S(1)}, u32[]{:S(2)}, u32[]{:S(2)}) %all-to-all-start.1) | async-done | bytes 1048608 | tf_op jit(solution)/shard_map/all_to_all | solution.py:53
  57.0 0.1 copy.40
  57.1 30.3 %while.10 = (s32[]{:T(128)}, f32[8,2,16,1024]{3,2,1,0:T(8,128)S(1)}, s32[]{:T(128)}, s32[8,1,1,1]{0,3,2,1:T(1,128)S(1)}, f32[16,1024]{1,0:T(8,128)S(1)}, /*index=5*/s32[]{:T(128)}) while((s32[]{:T(128)}, f32[8,2,16,1024]{3,2,1,0:T(8,128)S(1)}, s32[]{:T(128)}, s32[8,1,1,1]{0,3,2,1:T(1,128)S(1)}, f32[16,1024]{1,0:T(8,128)S(1)}, ...), condition=%wide.region_3.4_spmd, body=%wide.region_2.3_spmd.sunk | while | flops 7864330 | bytes 4653177 | solution.py:32
  57.9 0.1 copy.52
  58.0 0.1 fusion.29
  58.1 1.3 add_select_fusion.2
  60.1 0.1 copy.52
  60.2 0.1 fusion.29
  60.4 1.3 add_select_fusion.2
  62.5 0.1 fusion.29
  62.6 1.3 add_select_fusion.2
  64.7 0.1 copy.52
  64.8 0.1 fusion.29
  64.9 1.3 add_select_fusion.2
  67.0 0.1 copy.52
  67.1 0.1 fusion.29
  67.2 1.3 add_select_fusion.2
  69.2 0.1 copy.52
  69.3 0.1 fusion.29
  69.5 1.3 add_select_fusion.2
  71.6 0.1 fusion.29
  71.7 1.3 add_select_fusion.2
  73.8 0.1 copy.52
  73.9 0.1 fusion.29
  74.0 1.3 add_select_fusion.2
  76.1 0.1 copy.52
  76.2 0.1 fusion.29
  76.3 1.3 add_select_fusion.2
  78.4 0.1 copy.52
  78.5 0.1 fusion.29
  78.6 1.3 add_select_fusion.2
  80.7 0.1 fusion.29
  80.9 1.3 add_select_fusion.2
  82.9 0.1 copy.52
  83.0 0.1 fusion.29
  83.1 1.3 add_select_fusion.2
  85.2 0.1 copy.52
  85.3 0.1 fusion.29
  85.4 1.3 add_select_fusion.2
  87.5 8.7 %copy.27 = f32[8,2,16,1024]{2,1,0,3:T(2,128)} copy(f32[8,2,16,1024]{3,2,1,0:T(8,128)S(1)} %get-tuple-element.33) | data formatting | bytes 2097152 | tf_op jit(solution)/shard_map/while | solution.py:32
  96.2 12.9 %reshape.37 = f32[8,1,32768]{2,1,0:T(1,128)S(1)} reshape(f32[1024,8,2,16]{3,2,1,0:T(2,128)} %bitcast.45) | data formatting | bytes 2097152
  109.0 43.4 %all_to_all.73 = f32[8,1,32768]{2,1,0:T(1,128)S(1)} all-to-all(f32[8,1,32768]{2,1,0:T(1,128)S(1)} %reshape.37), channel_id=1, replica_groups=mesh['lat'=2,'lon'=8,'mem'=32] {'lon'}, dimensions={0} | all-to-all | bytes 2097152 | tf_op jit(solution)/shard_map/all_to_all | solution.py:64
  152.4 0.5 broadcast.68
  152.9 3.2 reduce
  156.1 14.2 %reshape.38 = f32[1024,8,2,16]{3,2,1,0:T(2,128)} reshape(f32[8,32768]{1,0:T(8,128)S(1)} %reduce) | data formatting | bytes 2097152
  170.3 10.2 %copy.35 = f32[8,2,16,8,128]{4,2,1,0,3:T(8,128)S(1)} copy(f32[8,2,16,8,128]{2,1,0,4,3:T(2,128)} %bitcast.46) | data formatting | bytes 2097152 | tf_op jit(solution)/shard_map/all_to_all | solution.py:64
  180.5 0.5 copy.30
  181.1 4.2 %all_to_all.74 = f32[64,2,16,128]{3,1,0,2:T(2,128)S(1)} all-to-all(f32[64,2,16,128]{3,1,0,2:T(2,128)S(1)} %copy.30), channel_id=1, replica_groups=mesh['lat'=2,'lon'=8,'mem'=32] {'lat'}, dimensions={2} | all-to-all | bytes 2097152 | tf_op jit(solution)/shard_map/all_to_all | solution.py:65
  185.3 0.6 copy.41
  186.0 0.2 fusion.13
  186.2 0.8 broadcast_multiply_fusion
  187.1 210.9 %reduce-scatter.2.cloned.1.call-done = f32[4,8,128]{2,1,0:T(8,128)} async-done(((f32[128,8,128]{2,1,0:T(8,128)}), f32[4,8,128]{2,1,0:T(8,128)}) %reduce-scatter.2.cloned.1.call-update) | async-done | bytes 16400 | tf_op jit(solution)/shard_map/reduce_scatter | solution.py:68
  (29 shorter events, 0.6 us)
Async XLA Ops:
  6.5 21.4 %copy-start = (s32[128]{0:T(128)S(1)}, s32[128]{0:T(128)}, u32[]{:S(2)}) copy-start(s32[128]{0:T(128)} %param.11) | copy-start | bytes 1540
  6.5 22.9 %copy-start.2 = (f32[16,1024]{1,0:T(8,128)S(1)}, f32[16,1024]{1,0:T(8,128)}, u32[]{:S(2)}) copy-start(f32[16,1024]{1,0:T(8,128)} %param.9) | copy-start | bytes 196612
  24.2 32.8 %all-to-all-start.1 = ((f32[64,2,16,128]{3,2,1,0:T(8,128)}), f32[64,2,16,128]{3,2,1,0:T(8,128)S(1)}, u32[]{:S(2)}, u32[]{:S(2)}) async-start(f32[64,2,16,128]{3,2,1,0:T(8,128)} %bitcast.41), calls=%async_computation.1 | async-start | bytes 2097152 | tf_op jit(solution)/shard_map/all_to_all | solution.py:53
  27.8 370.2 %reduce-scatter.2.cloned.1.call-start = ((), (), s32[]{:S(2)}) async-start(), calls=%async_computation.5 | async-start | bytes 540672 | tf_op jit(solution)/shard_map/reduce_scatter | solution.py:68
  170.3 15.7 %copy-start.1 = (bf16[128,2,8,128]{3,2,1,0:T(8,128)(2,1)S(1)}, bf16[128,2,8,128]{3,2,1,0:T(8,128)(2,1)}, u32[]{:S(2)}) copy-start(bf16[128,2,8,128]{3,2,1,0:T(8,128)(2,1)} %param.8) | copy-start | bytes 1572868
Sparse Core Ops, SparseCore 0:
  187.2 210.7 reduce-scatter.1
where the time goes:
time: 410 us; the launch traced here: 405 us
  waiting for transfers between devices  239 us (58%)
  blocking collectives  58.7 us (14%)
  local copies, waits for them, and re-layouts  55 us (13%)
  other arithmetic  24.2 us (6%)
  between operations  13.5 us (3%)
  loops' own time  10.2 us (2%)
    reduce_scatter x1, waiting for transfers between devices, body(): lax.psum_scatter(partial_value, 'mem', scatter_dimension=0, tiled=True)  211 us
    all_to_all x1, blocking collectives, body(): lax.all_to_all(smoothed, 'lon', split_axis=3, concat_axis=0, tiled=True)  43.4 us
    all_to_all x1, waiting for transfers between devices, body(): lax.all_to_all(lax.all_to_all(vertical, 'lat', split_axis=0, concat_axis=...  27.6 us
    unnamed x8, local copies, waits for them, and re-layouts  27.1 us
    select_n x13, other arithmetic, one_step(): return jnp.where(step_index < active_counts, updated, state_now)  17.4 us
    all_to_all x3, local copies, waits for them, and re-layouts, body(): lax.all_to_all(smoothed, 'lon', split_axis=3, concat_axis=0, tiled=True)  11.3 us
    all_to_all x1, blocking collectives, body(): lax.all_to_all(vertical, 'lat', split_axis=0, concat_axis=2, tiled=True)  11.1 us
    another operation x1, loops' own time, diffuse_all(): return lax.fori_loop(0, limit, one_step, values_in)  10.2 us
  transfers between devices with their start and end apart: 2, of which 2 were waited for; matrix products, arithmetic and copies ran while one was open for 0% of the time, Pallas kernels for 0%

commit v1 on v0

v1 whole, which is shorter than its diff:
```python
import jax
import jax.numpy as jnp
from jax import lax
from jax.experimental import pallas as pl
from jax.experimental.pallas import tpu as pltpu
from jax.sharding import PartitionSpec as P

F32 = jnp.float32
BF16 = jnp.bfloat16
HALO = 24
TILE = 128
EXT = TILE + 2 * HALO
NJ = EXT // 8
ROWS = 16
MAX_STEPS = 24
NX = 4
NZ = 8
LON = 8


def iota(shape, dim):
    return lax.broadcasted_iota(jnp.int32, shape, dim)


def split2(value):
    high = value.astype(BF16)
    low = (value - high.astype(F32)).astype(BF16)
    return high, low


def dot(a, b):
    return jnp.dot(a, b, preferred_element_type=F32)


def diffuse_step(src, dst, cf, af, active, lclamp, rclamp, block):
    def body(b, carry):
        y0 = b * block
        above = jnp.maximum(y0 - 1, 0)
        below = jnp.minimum(y0 + block, ROWS - 1)
        ys = [y0 + i for i in range(block)]

        def load(y, j):
            return src[y, j * 8 : (j + 1) * 8, :]

        left = [pltpu.roll(load(y, NJ - 1), 1, 0) for y in ys]
        here = [load(y, 0) for y in ys]
        for j in range(NJ):
            if j < NJ - 1:
                right = [load(y, j + 1) for y in ys]
            else:
                right = [pltpu.roll(load(y, 0), 7, 0) for y in ys]
            column = [load(above, j)] + here + [load(below, j)]
            for i, y in enumerate(ys):
                a, c = left[i], right[i]
                if j == HALO % NJ:
                    a = jnp.where(lclamp, here[i], a)
                if j == (HALO + TILE - 1) % NJ:
                    c = jnp.where(rclamp, here[i], c)
                beside = (a + c) + (column[i] + column[i + 2])
                new = af[y, j * 8 : (j + 1) * 8, :] * here[i] + cf[y, j * 8 : (j + 1) * 8, :] * beside
                dst[y, j * 8 : (j + 1) * 8, :] = jnp.where(active, new, here[i])
            left, here = here, right
        return carry

    lax.fori_loop(0, ROWS // block, body, 0)


def kernel(
    alpha_ref, perturb_ref, gain_ref, bands_ref, steps_ref, out_ref,
    whi, wlo, vext, sib, ub0, ub1, cf, af, gt, pf, pt, psend, smo, xs, xr, acc, zs, zr,
    hs_sem, hr_sem, ps_sem, pr_sem, xs_sem, xr_sem, zs_sem, zr_sem,
):
    h = lax.axis_index("lat")
    g = lax.axis_index("lon")
    mi = lax.axis_index("mem")
    z = mi // NX
    x = mi % NX
    oh = 1 - h
    gl = lax.rem(g + LON - 1, LON)
    gr = lax.rem(g + 1, LON)

    def xmem(d):
        return z * NX + lax.rem(x + d, NX)

    def zmem(d):
        return lax.rem(z + d, NZ) * NX + x

    partners = [(oh, g, mi)]
    partners += [(a, b, mi) for a in (h, oh) for b in (gl, gr)]
    partners += [(h, g, xmem(d)) for d in range(1, NX)]
    partners += [(a, g, zmem(d)) for a in (h, oh) for d in range(1, NZ)]
    barrier = pltpu.get_barrier_semaphore()
    for p in partners:
        pl.semaphore_signal(barrier, inc=1, device_id=p, device_id_type=pl.DeviceIdType.MESH)

    def remote(src, dst, ssem, rsem, dev):
        return pltpu.make_async_remote_copy(
            src_ref=src, dst_ref=dst, send_sem=ssem, recv_sem=rsem,
            device_id=dev, device_id_type=pl.DeviceIdType.MESH,
        )

    n = iota((128, 256), 1)
    k = iota((128, 256), 0)
    core = lax.rem(h + n // 128, 2)
    member = lax.rem(n // 64, 2)
    q = lax.rem(n, 64)
    level = lax.rem(q, 8) * 16 + (q // 16) * 4 + core * 2 + lax.rem(q // 8, 2)
    onehot = jnp.where(k == level, 1.0, 0.0).astype(BF16)
    r8 = iota((8, 128), 0)
    rows = jnp.where(
        r8 == 0,
        jnp.broadcast_to(bands_ref[...].astype(F32), (8, 128)),
        jnp.broadcast_to(steps_ref[...].astype(F32), (8, 128)),
    ).astype(BF16)
    permuted = dot(rows, onehot)
    width = jnp.broadcast_to(permuted[0:1, :], (128, 256))
    count = jnp.broadcast_to(permuted[1:2, 0:128], (8, 128))
    distance = jnp.abs(k - level).astype(F32)
    raw = jnp.where(distance <= width, 1.0 - distance / (width + 1.0), 0.0)
    weights = raw / jnp.sum(raw, axis=0, keepdims=True)
    for m in range(2):
        high, low = split2(jnp.where(member == m, weights, 0.0))
        whi[m * 128 : (m + 1) * 128, :] = high
        wlo[m * 128 : (m + 1) * 128, :] = low

    def vertical(y, carry):
        a0 = alpha_ref[pl.ds(y, 128, stride=16), :]
        a1 = alpha_ref[pl.ds(y + 8, 128, stride=16), :]
        high, low = split2(jnp.concatenate([a0.T, a1.T], axis=1))
        w = whi[...]
        v = dot(high, w) + dot(low, w) + dot(high, wlo[...])
        vext[h * 8 + y, HALO : HALO + TILE, :] = v[:, 0:128]
        sib[y] = v[:, 128:256]
        return carry

    halo_copies = []
    for b in range(2):
        lax.fori_loop(4 * b, 4 * b + 4, vertical, 0)
        if b == 0:
            pl.semaphore_wait(barrier, len(partners))
        own_rows = pl.ds(h * 8 + 4 * b, 4)
        sib_rows = pl.ds(4 * b, 4)
        lefts = pl.ds(0, HALO)
        rights = pl.ds(HALO + TILE, HALO)
        sends = [
            (vext.at[own_rows, pl.ds(HALO, HALO)], vext.at[own_rows, rights], (h, gl, mi)),
            (vext.at[own_rows, pl.ds(TILE, HALO)], vext.at[own_rows, lefts], (h, gr, mi)),
            (sib.at[sib_rows, pl.ds(0, HALO)], vext.at[own_rows, rights], (oh, gl, mi)),
            (sib.at[sib_rows, pl.ds(TILE - HALO, HALO)], vext.at[own_rows, lefts], (oh, gr, mi)),
            (sib.at[sib_rows], vext.at[own_rows, pl.ds(HALO, TILE)], (oh, g, mi)),
        ]
        for i, (src, dst, dev) in enumerate(sends):
            cp = remote(src, dst, hs_sem.at[b, i], hr_sem.at[b, i], dev)
            cp.start()
            halo_copies.append(cp)

    def widen(i, carry):
        at = pl.ds(pl.multiple_of(i * 256, 256), 256)
        pf[at, :] = perturb_ref[at, :].astype(F32)
        return carry

    lax.fori_loop(0, 8, widen, 0)

    def pick(y, c):
        parts = []
        for m in range(2):
            for xx in range(NX):
                for lv in range(2):
                    parts.append(pf[pl.ds(xx * 64 + c * 32 + lv * 16 + m * 8 + y, 8, stride=256), :])
        return jnp.concatenate(parts, axis=0).astype(BF16)

    def pick_other(y, carry):
        psend[y] = pick(y, oh)
        return carry

    def pick_own(y, carry):
        pt[h * 8 + y] = pick(y, h)
        return carry

    lax.fori_loop(0, 8, pick_other, 0)
    pcopy = remote(psend, pt.at[pl.ds(h * 8, 8)], ps_sem.at[0], pr_sem.at[0], (oh, g, mi))
    pcopy.start()
    lax.fori_loop(0, 8, pick_own, 0)

    def gain_tile(t):
        tile = gain_ref[:, pl.ds(pl.multiple_of(t * TILE, TILE), TILE)]
        return (0.24 * jnp.concatenate([tile, jnp.zeros((TILE - ROWS, TILE), F32)], axis=0)).T

    gt[0:HALO, :] = gain_tile(gl)[TILE - HALO :, :]
    gt[HALO : HALO + TILE, :] = gain_tile(g)
    gt[HALO + TILE :, :] = gain_tile(gr)[:HALO, :]
    gp = jnp.concatenate([gt[pl.ds(j, 8, stride=NJ), :] for j in range(NJ)], axis=0)
    g1 = gp.astype(BF16).astype(F32)
    g2 = (gp - g1).astype(BF16).astype(F32)
    g3 = gp - g1 - g2
    gsplit = (g1 + pltpu.roll(g2, 16, 1) + pltpu.roll(g3, 32, 1)).astype(BF16)
    rr = iota((128, 128), 0)

    def spread(y, carry):
        pickrow = jnp.where(jnp.logical_and(rr < 48, lax.rem(rr, 16) == y), 1.0, 0.0).astype(BF16)
        c = dot(gsplit, pickrow)
        cf[y] = c
        af[y] = 1.0 - 4.0 * c
        return carry

    lax.fori_loop(0, ROWS, spread, 0)

    for cp in halo_copies:
        cp.wait_recv()

    def restride(y, carry):
        for j in range(NJ):
            ub0[y, j * 8 : (j + 1) * 8, :] = vext[y, pl.ds(j, 8, stride=NJ), :]
        return carry

    lax.fori_loop(0, ROWS, restride, 0)

    sub = iota((8, 128), 0)
    lclamp = jnp.logical_and(sub == HALO // NJ, g == 0)
    rclamp = jnp.logical_and(sub == (HALO + TILE - 1) // NJ, g == LON - 1)

    def two_steps(s, carry):
        t = (2 * s).astype(F32)
        diffuse_step(ub0, ub1, cf, af, t < count, lclamp, rclamp, 8)
        diffuse_step(ub1, ub0, cf, af, t + 1.0 < count, lclamp, rclamp, 8)
        return carry

    lax.fori_loop(0, MAX_STEPS // 2, two_steps, 0)

    pcopy.wait_recv()

    def weigh(y, carry):
        for j in range(NJ):
            smo[pl.ds(j, 8, stride=NJ), :] = ub0[y, j * 8 : (j + 1) * 8, :]
        product = smo[HALO : HALO + TILE, :].T * pt[y].astype(F32)
        total = (product[0:64, :] + product[64:128, :]) * 0.125
        for xx in range(NX):
            xs[xx, y] = total[xx * 16 : (xx + 1) * 16, :]
        return carry

    xcopies = []
    for b in range(2):
        lax.fori_loop(8 * b, 8 * b + 8, weigh, 0)
        half = pl.ds(8 * b, 8)
        for d in range(1, NX):
            cp = remote(
                xs.at[lax.rem(x + d, NX), half], xr.at[d - 1, half],
                xs_sem.at[b, d - 1], xr_sem.at[b, d - 1], (h, g, xmem(d)),
            )
            cp.start()
            xcopies.append(cp)

    for cp in xcopies:
        cp.wait_recv()

    def gather(y, carry):
        acc[pl.ds(pl.multiple_of(y * 16, 16), 16), :] = (xs[x, y] + xr[0, y]) + (xr[1, y] + xr[2, y])
        return carry

    lax.fori_loop(0, ROWS, gather, 0)

    for zz in range(NZ):
        for hh in range(2):
            for lv in range(2):
                zs[zz, hh, lv] = acc[pl.ds(hh * 128 + lv * 8 + zz, 8, stride=16), :]

    zcopies = []
    for d in range(NZ):
        for e in range(2):
            if d == 0 and e == 0:
                continue
            cp = remote(
                zs.at[lax.rem(z + d, NZ), lax.rem(h + e, 2)], zr.at[d * 2 + e],
                zs_sem.at[d * 2 + e], zr_sem.at[d * 2 + e], (lax.rem(h + e, 2), g, zmem(d)),
            )
            cp.start()
            zcopies.append(cp)
    for cp in zcopies:
        cp.wait_recv()
    same = zs[z, h]
    other = zr[1]
    for d in range(1, NZ):
        same = same + zr[2 * d]
        other = other + zr[2 * d + 1]
    out_ref[pl.ds(2 * h, 2)] = same
    out_ref[pl.ds(2 * oh, 2)] = other

    for cp in halo_copies + [pcopy] + xcopies + zcopies:
        cp.wait_send()


def body(alpha, perturb, smooth_gain, bands, steps):
    vmem = pl.BlockSpec(memory_space=pltpu.VMEM)
    dma = pltpu.SemaphoreType.DMA
    return pl.pallas_call(
        kernel,
        out_shape=jax.ShapeDtypeStruct((4, 8, TILE), F32),
        in_specs=[vmem] * 5,
        out_specs=vmem,
        scratch_shapes=[
            pltpu.VMEM((256, 256), BF16),
            pltpu.VMEM((256, 256), BF16),
            pltpu.VMEM((ROWS, EXT, 128), F32),
            pltpu.VMEM((8, TILE, 128), F32),
            pltpu.VMEM((ROWS, EXT, 128), F32),
            pltpu.VMEM((ROWS, EXT, 128), F32),
            pltpu.VMEM((ROWS, EXT, 128), F32),
            pltpu.VMEM((ROWS, EXT, 128), F32),
            pltpu.VMEM((EXT, 128), F32),
            pltpu.VMEM((2048, 128), F32),
            pltpu.VMEM((ROWS, 128, TILE), BF16),
            pltpu.VMEM((8, 128, TILE), BF16),
            pltpu.VMEM((EXT, 128), F32),
            pltpu.VMEM((NX, ROWS, 16, TILE), F32),
            pltpu.VMEM((NX - 1, ROWS, 16, TILE), F32),
            pltpu.VMEM((256, TILE), F32),
            pltpu.VMEM((NZ, 2, 2, 8, TILE), F32),
            pltpu.VMEM((2 * NZ, 2, 8, TILE), F32),
            dma((2, 5)), dma((2, 5)), dma((1,)), dma((1,)),
            dma((2, 3)), dma((2, 3)), dma((16,)), dma((16,)),
        ],
        compiler_params=pltpu.CompilerParams(
            collective_id=0, has_side_effects=True, vmem_limit_bytes=48 << 20
        ),
    )(
        alpha.reshape(2048, TILE),
        perturb.reshape(2048, TILE),
        smooth_gain,
        bands.reshape(1, 128),
        steps.reshape(1, 128),
    )


def solution(mesh):
    placed = (P(None, "mem", "lat", "lon"), P(None, "mem", "lat", "lon"), P(), P(), P())
    return jax.shard_map(
        body, mesh=mesh, in_specs=placed, out_specs=P("mem", "lat", "lon"), check_vma=False
    )
```

time: 410 us -> 50 us (0.12); the launches traced: 405 us -> 49.7 us
  waiting for transfers between devices: 239 us -> 0 us
  blocking collectives: 58.7 us -> 0 us
  local copies, waits for them, and re-layouts: 55 us -> 4.38 us
  Pallas kernels: 0 us -> 45.3 us
  other arithmetic: 24.2 us -> 0 us
  between operations: 13.5 us -> 0.01 us
  loops' own time: 10.2 us -> 0 us
    reduce_scatter x1 -> x0, waiting for transfers between devices: 211 us -> none  [body(): lax.psum_scatter(partial_value, 'mem', scatter_dimension=0, tiled=True)]
    all_to_all x3 -> x0, blocking collectives: 58.7 us -> none  [the longest x1 43.4 us: body(): lax.all_to_all(smoothed, 'lon', split_axis=3, concat_axis=0, tiled=True)]
    pallas_call x0 -> x1, Pallas kernels: none -> 45.3 us  [body(): pl.pallas_call(kernel, out_shape=jax.ShapeDtypeStruct((4, 8, TILE), F32),...]
    all_to_all x1 -> x0, waiting for transfers between devices: 27.6 us -> none  [body(): lax.all_to_all(lax.all_to_all(vertical, 'lat', split_axis=0, concat_axis=...]
    unnamed x8 -> x11, local copies, waits for them, and re-layouts: 27.1 us -> 4.38 us
    select_n x14 -> x0, other arithmetic: 17.5 us -> none  [the longest x13 17.4 us: one_step(): return jnp.where(step_index < active_counts, updated, state_now)]
    all_to_all x7 -> x0, local copies, waits for them, and re-layouts: 13.2 us -> none  [the longest x3 11.3 us: body(): lax.all_to_all(smoothed, 'lon', split_axis=3, concat_axis=0, tiled=True)]
    another operation x1 -> x0, loops' own time: 10.2 us -> none  [diffuse_all(): return lax.fori_loop(0, limit, one_step, values_in)]
  transfers between devices with their start and end apart: 2 -> 0, of which waited for: 2 -> 0; matrix products, arithmetic and copies ran while one was open for 0% -> 0% of each run, Pallas kernels for 0% -> 0%
where the time goes in v1:
time: 50 us; the launch traced here: 49.7 us
  Pallas kernels  45.3 us (91%)
  local copies, waits for them, and re-layouts  4.38 us (9%)
    pallas_call x1, Pallas kernels, body(): pl.pallas_call(kernel, out_shape=jax.ShapeDtypeStruct((4, 8, TILE), F32),...  45.3 us
    unnamed x11, local copies, waits for them, and re-layouts  4.38 us

profile of v1, /device:TPU:1, one launch (start us, length us, event | category | flops | bytes accessed | tf_op | source)
XLA Modules:
  0.0 49.7 jit_solution(2757300025949510367)
XLA Ops:
  0.0 0.0 copy-start.3
  0.0 0.0 copy-start.4
  0.0 0.7 %copy-done.3 = s32[128]{0:T(128)S(1)} copy-done((s32[128]{0:T(128)S(1)}, s32[128]{0:T(128)}, u32[]{:S(2)}) %copy-start.3) | copy-done | bytes 536
  0.7 0.0 copy-done.4
  0.7 0.0 copy-start
  0.7 1.2 %copy-done = f32[128,2,8,128]{3,2,1,0:T(8,128)S(1)} copy-done((f32[128,2,8,128]{3,2,1,0:T(8,128)S(1)}, f32[128,2,8,128]{3,2,1,0:T(8,128)}, u32[]{:S(2)}) %copy-start) | copy-done | bytes 1048600
  1.9 0.0 copy-start.1
  1.9 1.0 %copy-done.1 = bf16[128,2,8,128]{3,2,1,0:T(8,128)(2,1)S(1)} copy-done((bf16[128,2,8,128]{3,2,1,0:T(8,128)(2,1)S(1)}, bf16[128,2,8,128]{3,2,1,0:T(8,128)(2,1)}, u32[]{:S(2)}) %copy-start.1) | copy-done | bytes 524312
  2.9 0.0 copy-start.2
  2.9 0.8 %copy-done.2 = f32[16,1024]{1,0:T(8,128)S(1)} copy-done((f32[16,1024]{1,0:T(8,128)S(1)}, f32[16,1024]{1,0:T(8,128)}, u32[]{:S(2)}) %copy-start.2) | copy-done | bytes 65560
  3.8 45.3 %shard_map.55 = f32[4,8,128]{2,1,0:T(8,128)S(1)} custom-call(f32[2048,128]{1,0:T(8,128)S(1)} %bitcast.4, bf16[2048,128]{1,0:T(8,128)(2,1)S(1)} %bitcast.5, f32[16,1024]{1,0:T(8,128)S(1)} %copy-done.2, s32[1,128]{1,0:T(1,128)S(1)} %bitcast.6, s32[1,128]{1,0:T(1,128)S(1)} %bitcast.7), custom_call_target="tpu_custom_call" | custom-call | tf_op jit(solution)/shard_map/pallas_call | solution.py:295
  49.1 0.6 %copy.7 = f32[4,8,128]{2,1,0:T(8,128)} copy(f32[4,8,128]{2,1,0:T(8,128)S(1)} %shard_map.55) | data formatting | bytes 32768
Async XLA Ops:
  0.0 0.7 %copy-start.3 = (s32[128]{0:T(128)S(1)}, s32[128]{0:T(128)}, u32[]{:S(2)}) copy-start(s32[128]{0:T(128)} %param.8) | copy-start | bytes 1540
  0.0 0.7 %copy-start.4 = (s32[128]{0:T(128)S(1)}, s32[128]{0:T(128)}, u32[]{:S(2)}) copy-start(s32[128]{0:T(128)} %param.9) | copy-start | bytes 1540
  0.7 1.2 %copy-start = (f32[128,2,8,128]{3,2,1,0:T(8,128)S(1)}, f32[128,2,8,128]{3,2,1,0:T(8,128)}, u32[]{:S(2)}) copy-start(f32[128,2,8,128]{3,2,1,0:T(8,128)} %param.5) | copy-start | bytes 3145732
  1.9 1.0 %copy-start.1 = (bf16[128,2,8,128]{3,2,1,0:T(8,128)(2,1)S(1)}, bf16[128,2,8,128]{3,2,1,0:T(8,128)(2,1)}, u32[]{:S(2)}) copy-start(bf16[128,2,8,128]{3,2,1,0:T(8,128)(2,1)} %param.6) | copy-start | bytes 1572868
  2.9 0.8 %copy-start.2 = (f32[16,1024]{1,0:T(8,128)S(1)}, f32[16,1024]{1,0:T(8,128)}, u32[]{:S(2)}) copy-start(f32[16,1024]{1,0:T(8,128)} %gain_ref.1) | copy-start | bytes 196612

commit v2 on v1

v2 whole, which is shorter than its diff:
```python
import jax
import jax.numpy as jnp
from jax import lax
from jax.experimental import pallas as pl
from jax.experimental.pallas import tpu as pltpu
from jax.sharding import PartitionSpec as P

F32 = jnp.float32
BF16 = jnp.bfloat16
HALO = 24
TILE = 128
EXT = TILE + 2 * HALO
NJ = EXT // 8
ROWS = 16
MAX_STEPS = 24
NX = 4
NZ = 8
LON = 8


def iota(shape, dim):
    return lax.broadcasted_iota(jnp.int32, shape, dim)


def split2(value):
    high = value.astype(BF16)
    low = (value - high.astype(F32)).astype(BF16)
    return high, low


def dot(a, b):
    return jnp.dot(a, b, preferred_element_type=F32)


def diffuse_step(src, dst, cf, af, active, lclamp, rclamp, block):
    def body(b, carry):
        y0 = b * block
        above = jnp.maximum(y0 - 1, 0)
        below = jnp.minimum(y0 + block, ROWS - 1)
        ys = [y0 + i for i in range(block)]

        def load(y, j):
            return src[y, j * 8 : (j + 1) * 8, :]

        left = [pltpu.roll(load(y, NJ - 1), 1, 0) for y in ys]
        here = [load(y, 0) for y in ys]
        pairs = None
        for j in range(NJ):
            if j < NJ - 1:
                right = [load(y, j + 1) for y in ys]
            else:
                right = [pltpu.roll(load(y, 0), 7, 0) for y in ys]
            top, bottom = load(above, j), load(below, j)
            if j == HALO % NJ:
                left = [jnp.where(lclamp, u, a) for u, a in zip(here, left)]
            if pairs is None or j == HALO % NJ:
                up_left = [u + a for u, a in zip([top] + here[:-1], left)]
            else:
                up_left = [top + left[0]] + pairs[:-1]
            beyond = right
            if j == (HALO + TILE - 1) % NJ:
                beyond = [jnp.where(rclamp, u, a) for u, a in zip(here, right)]
            pairs = [d + r for d, r in zip(here[1:] + [bottom], beyond)]
            for i, y in enumerate(ys):
                at = (y, slice(j * 8, (j + 1) * 8), slice(None))
                new = af[at] * here[i] + cf[at] * (up_left[i] + pairs[i])
                dst[at] = jnp.where(active, new, here[i])
            left, here = here, right
        return carry

    lax.fori_loop(0, ROWS // block, body, 0)


def kernel(
    alpha_hbm, perturb_hbm, gain_hbm, bands_hbm, steps_hbm, out_ref,
    alpha_ref, perturb_ref, gain_ref, bands_ref, steps_ref,
    whi, wlo, vext, sib, hsend, hrecv, ub0, ub1, cf, af, gt, pf, pt, psend, smo, xs, xr, acc, zs, zr,
    in_sem, hs_sem, hr_sem, ps_sem, pr_sem, xs_sem, xr_sem, zs_sem, zr_sem,
):
    h = lax.axis_index("lat")
    g = lax.axis_index("lon")
    mi = lax.axis_index("mem")
    z = mi // NX
    x = mi % NX
    oh = 1 - h
    gl = lax.rem(g + LON - 1, LON)
    gr = lax.rem(g + 1, LON)

    def xmem(d):
        return z * NX + lax.rem(x + d, NX)

    def zmem(d):
        return lax.rem(z + d, NZ) * NX + x

    partners = [(oh, g, mi)]
    partners += [(a, b, mi) for a in (h, oh) for b in (gl, gr)]
    partners += [(h, g, xmem(d)) for d in range(1, NX)]
    partners += [(a, g, zmem(d)) for a in (h, oh) for d in range(1, NZ)]
    barrier = pltpu.get_barrier_semaphore()
    for p in partners:
        pl.semaphore_signal(barrier, inc=1, device_id=p, device_id_type=pl.DeviceIdType.MESH)

    loads = [
        pltpu.make_async_copy(bands_hbm, bands_ref, in_sem.at[0]),
        pltpu.make_async_copy(steps_hbm, steps_ref, in_sem.at[1]),
    ]
    for i in range(4):
        part = pl.ds(i * 512, 512)
        loads.append(pltpu.make_async_copy(alpha_hbm.at[part], alpha_ref.at[part], in_sem.at[2 + i]))
    loads.append(pltpu.make_async_copy(gain_hbm, gain_ref, in_sem.at[6]))
    loads.append(pltpu.make_async_copy(perturb_hbm, perturb_ref, in_sem.at[7]))
    for cp in loads:
        cp.start()

    def remote(src, dst, ssem, rsem, dev):
        return pltpu.make_async_remote_copy(
            src_ref=src, dst_ref=dst, send_sem=ssem, recv_sem=rsem,
            device_id=dev, device_id_type=pl.DeviceIdType.MESH,
        )

    loads[0].wait()
    loads[1].wait()
    n = iota((128, 256), 1)
    k = iota((128, 256), 0)
    core = lax.rem(h + n // 128, 2)
    member = lax.rem(n // 64, 2)
    q = lax.rem(n, 64)
    level = lax.rem(q, 8) * 16 + (q // 16) * 4 + core * 2 + lax.rem(q // 8, 2)
    onehot = jnp.where(k == level, 1.0, 0.0).astype(BF16)
    r8 = iota((8, 128), 0)
    rows = jnp.where(
        r8 == 0,
        jnp.broadcast_to(bands_ref[...].astype(F32), (8, 128)),
        jnp.broadcast_to(steps_ref[...].astype(F32), (8, 128)),
    ).astype(BF16)
    permuted = dot(rows, onehot)
    width = jnp.broadcast_to(permuted[0:1, :], (128, 256))
    count = jnp.broadcast_to(permuted[1:2, 0:128], (8, 128))
    distance = jnp.abs(k - level).astype(F32)
    raw = jnp.where(distance <= width, 1.0 - distance / (width + 1.0), 0.0)
    weights = raw / jnp.sum(raw, axis=0, keepdims=True)
    for m in range(2):
        high, low = split2(jnp.where(member == m, weights, 0.0))
        whi[m * 128 : (m + 1) * 128, :] = high
        wlo[m * 128 : (m + 1) * 128, :] = low

    def vertical(p, carry):
        turned = []
        for i in range(2):
            y = 2 * p + i
            a0 = alpha_ref[pl.ds(y, 128, stride=16), :]
            a1 = alpha_ref[pl.ds(y + 8, 128, stride=16), :]
            turned.append(jnp.concatenate([a0.T, a1.T], axis=1))
        high, low = split2(jnp.concatenate(turned, axis=0))
        w = whi[...]
        v = dot(high, w) + dot(low, w) + dot(high, wlo[...])
        for i in range(2):
            vext[h * 8 + 2 * p + i, HALO : HALO + TILE, :] = v[i * TILE : (i + 1) * TILE, 0:128]
            sib[2 * p + i] = v[i * TILE : (i + 1) * TILE, 128:256]
        for core in range(2):
            c = v[:, core * 128 : (core + 1) * 128]
            for side, x0 in enumerate((0, TILE - HALO)):
                hsend[core, side, p] = jnp.concatenate(
                    [c[x0 : x0 + HALO], c[TILE + x0 : TILE + x0 + HALO]], axis=0
                ).astype(BF16)
        return carry

    for cp in loads[2:6]:
        cp.wait()
    halo_copies = []
    for b in range(2):
        lax.fori_loop(2 * b, 2 * b + 2, vertical, 0)
        if b == 0:
            pl.semaphore_wait(barrier, len(partners))
        own_pairs = pl.ds(h * 4 + 2 * b, 2)
        pairs = pl.ds(2 * b, 2)
        sends = [
            (hsend.at[0, 0, pairs], hrecv.at[1, own_pairs], (h, gl, mi)),
            (hsend.at[0, 1, pairs], hrecv.at[0, own_pairs], (h, gr, mi)),
            (hsend.at[1, 0, pairs], hrecv.at[1, own_pairs], (oh, gl, mi)),
            (hsend.at[1, 1, pairs], hrecv.at[0, own_pairs], (oh, gr, mi)),
            (sib.at[pl.ds(4 * b, 4)], vext.at[pl.ds(h * 8 + 4 * b, 4), pl.ds(HALO, TILE)], (oh, g, mi)),
        ]
        for i, (src, dst, dev) in enumerate(sends):
            cp = remote(src, dst, hs_sem.at[b, i], hr_sem.at[b, i], dev)
            cp.start()
            halo_copies.append(cp)

    def widen(i, carry):
        at = pl.ds(pl.multiple_of(i * 256, 256), 256)
        pf[at, :] = perturb_ref[at, :].astype(F32)
        return carry

    loads[7].wait()
    lax.fori_loop(0, 8, widen, 0)

    def pick(y, c):
        parts = []
        for m in range(2):
            for xx in range(NX):
                for lv in range(2):
                    parts.append(pf[pl.ds(xx * 64 + c * 32 + lv * 16 + m * 8 + y, 8, stride=256), :])
        return jnp.concatenate(parts, axis=0).astype(BF16)

    def pick_other(y, carry):
        psend[y] = pick(y, oh)
        return carry

    def pick_own(y, carry):
        pt[h * 8 + y] = pick(y, h)
        return carry

    lax.fori_loop(0, 8, pick_other, 0)
    pcopy = remote(psend, pt.at[pl.ds(h * 8, 8)], ps_sem.at[0], pr_sem.at[0], (oh, g, mi))
    pcopy.start()
    lax.fori_loop(0, 8, pick_own, 0)

    loads[6].wait()
    def gain_tile(t):
        tile = gain_ref[:, pl.ds(pl.multiple_of(t * TILE, TILE), TILE)]
        return (0.24 * jnp.concatenate([tile, jnp.zeros((TILE - ROWS, TILE), F32)], axis=0)).T

    gt[0:HALO, :] = gain_tile(gl)[TILE - HALO :, :]
    gt[HALO : HALO + TILE, :] = gain_tile(g)
    gt[HALO + TILE :, :] = gain_tile(gr)[:HALO, :]

    def spread(j, carry):
        columns = gt[pl.ds(j, 8, stride=NJ), :]
        at = pl.ds(pl.multiple_of(j * 8, 8), 8)
        for y in range(ROWS):
            c = jnp.broadcast_to(columns[:, y : y + 1], (8, 128))
            cf[y, at, :] = c
            af[y, at, :] = 1.0 - 4.0 * c
        return carry

    lax.fori_loop(0, NJ, spread, 0)

    for cp in halo_copies:
        cp.wait_recv()

    def restride(p, carry):
        lefts = hrecv[0, p].astype(F32)
        rights = hrecv[1, p].astype(F32)
        for i in range(2):
            y = 2 * p + i
            vext[y, 0:HALO, :] = lefts[i * HALO : (i + 1) * HALO]
            vext[y, HALO + TILE :, :] = rights[i * HALO : (i + 1) * HALO]
            for j in range(NJ):
                ub0[y, j * 8 : (j + 1) * 8, :] = vext[y, pl.ds(j, 8, stride=NJ), :]
        return carry

    lax.fori_loop(0, ROWS // 2, restride, 0)

    sub = iota((8, 128), 0)
    lclamp = jnp.logical_and(sub == HALO // NJ, g == 0)
    rclamp = jnp.logical_and(sub == (HALO + TILE - 1) // NJ, g == LON - 1)

    def two_steps(s, carry):
        t = (2 * s).astype(F32)
        diffuse_step(ub0, ub1, cf, af, t < count, lclamp, rclamp, 8)
        diffuse_step(ub1, ub0, cf, af, t + 1.0 < count, lclamp, rclamp, 8)
        return carry

    lax.fori_loop(0, MAX_STEPS // 2, two_steps, 0)

    pcopy.wait_recv()

    def weigh(i, base):
        for k in range(4):
            y = base + 4 * i + k
            for j in range(NJ):
                smo[k, pl.ds(j, 8, stride=NJ), :] = ub0[y, j * 8 : (j + 1) * 8, :]
        for k in range(4):
            y = base + 4 * i + k
            product = smo[k, HALO : HALO + TILE, :].T * pt[y].astype(F32)
            total = (product[0:64, :] + product[64:128, :]) * 0.125
            for xx in range(NX):
                xs[xx, y] = total[xx * 16 : (xx + 1) * 16, :]
        return base

    xcopies = []
    for e in (1, 0):
        base = 8 * lax.rem(h + e, 2)
        lax.fori_loop(0, 2, weigh, base)
        half = pl.ds(base, 8)
        group = []
        for d in range(1, NX):
            cp = remote(
                xs.at[lax.rem(x + d, NX), half], xr.at[d - 1, half],
                xs_sem.at[e, d - 1], xr_sem.at[e, d - 1], (h, g, xmem(d)),
            )
            cp.start()
            group.append(cp)
        xcopies.append(group)

    zcopies = []
    for e, group in zip((1, 0), xcopies):
        to = lax.rem(h + e, 2)
        base = 8 * to
        for cp in group:
            cp.wait_recv()

        def gather(i, carry):
            y = base + i
            acc[pl.ds(pl.multiple_of(y * 16, 16), 16), :] = (xs[x, y] + xr[0, y]) + (xr[1, y] + xr[2, y])
            return carry

        lax.fori_loop(0, 8, gather, 0)
        for zz in range(NZ):
            for lv in range(2):
                zs[zz, e, lv] = acc[pl.ds(to * 128 + lv * 8 + zz, 8, stride=16), :]
        for d in range(NZ):
            if d == 0 and e == 0:
                continue
            cp = remote(
                zs.at[lax.rem(z + d, NZ), e], zr.at[d * 2 + e],
                zs_sem.at[d * 2 + e], zr_sem.at[d * 2 + e], (to, g, zmem(d)),
            )
            cp.start()
            zcopies.append(cp)
    for cp in zcopies:
        cp.wait_recv()
    same = zs[z, 0]
    other = zr[1]
    for d in range(1, NZ):
        same = same + zr[2 * d]
        other = other + zr[2 * d + 1]
    out_ref[pl.ds(2 * h, 2)] = same
    out_ref[pl.ds(2 * oh, 2)] = other

    for cp in halo_copies + [pcopy] + xcopies[0] + xcopies[1] + zcopies:
        cp.wait_send()


def body(alpha, perturb, smooth_gain, bands, steps):
    vmem = pl.BlockSpec(memory_space=pltpu.VMEM)
    dma = pltpu.SemaphoreType.DMA
    return pl.pallas_call(
        kernel,
        out_shape=jax.ShapeDtypeStruct((4, 8, TILE), F32),
        in_specs=[pl.BlockSpec(memory_space=pl.ANY)] * 5,
        out_specs=vmem,
        scratch_shapes=[
            pltpu.VMEM((2048, TILE), F32),
            pltpu.VMEM((2048, TILE), BF16),
            pltpu.VMEM((ROWS, LON * TILE), F32),
            pltpu.VMEM((1, 128), jnp.int32),
            pltpu.VMEM((1, 128), jnp.int32),
            pltpu.VMEM((256, 256), BF16),
            pltpu.VMEM((256, 256), BF16),
            pltpu.VMEM((ROWS, EXT, 128), F32),
            pltpu.VMEM((8, TILE, 128), F32),
            pltpu.VMEM((2, 2, 4, 2 * HALO, 128), BF16),
            pltpu.VMEM((2, ROWS // 2, 2 * HALO, 128), BF16),
            pltpu.VMEM((ROWS, EXT, 128), F32),
            pltpu.VMEM((ROWS, EXT, 128), F32),
            pltpu.VMEM((ROWS, EXT, 128), F32),
            pltpu.VMEM((ROWS, EXT, 128), F32),
            pltpu.VMEM((EXT, 128), F32),
            pltpu.VMEM((2048, 128), F32),
            pltpu.VMEM((ROWS, 128, TILE), BF16),
            pltpu.VMEM((8, 128, TILE), BF16),
            pltpu.VMEM((4, EXT, 128), F32),
            pltpu.VMEM((NX, ROWS, 16, TILE), F32),
            pltpu.VMEM((NX - 1, ROWS, 16, TILE), F32),
            pltpu.VMEM((256, TILE), F32),
            pltpu.VMEM((NZ, 2, 2, 8, TILE), F32),
            pltpu.VMEM((2 * NZ, 2, 8, TILE), F32),
            dma((8,)), dma((2, 5)), dma((2, 5)), dma((1,)), dma((1,)),
            dma((2, 3)), dma((2, 3)), dma((16,)), dma((16,)),
        ],
        compiler_params=pltpu.CompilerParams(
            collective_id=0, has_side_effects=True, vmem_limit_bytes=60 << 20
        ),
    )(
        alpha.reshape(2048, TILE),
        perturb.reshape(2048, TILE),
        smooth_gain,
        bands.reshape(1, 128),
        steps.reshape(1, 128),
    )


def solution(mesh):
    placed = (P(None, "mem", "lat", "lon"), P(None, "mem", "lat", "lon"), P(), P(), P())
    return jax.shard_map(
        body, mesh=mesh, in_specs=placed, out_specs=P("mem", "lat", "lon"), check_vma=False
    )
```

time: 50 us -> 42.2 us (0.84)
  Pallas kernels: 45.3 us -> 40.7 us
  local copies, waits for them, and re-layouts: 4.38 us -> 1.32 us
    pallas_call x1, Pallas kernels: 45.3 us -> 40.7 us  [body(): pl.pallas_call(kernel, out_shape=jax.ShapeDtypeStruct((4, 8, TILE), F32),...]
    unnamed x11 -> x1, local copies, waits for them, and re-layouts: 4.38 us -> 1.32 us
where the time goes in v2:
time: 42.2 us; the launch traced here: 42 us
  Pallas kernels  40.7 us (96%)
  local copies, waits for them, and re-layouts  1.32 us (3%)
    pallas_call x1, Pallas kernels, body(): pl.pallas_call(kernel, out_shape=jax.ShapeDtypeStruct((4, 8, TILE), F32),...  40.7 us
    unnamed x1, local copies, waits for them, and re-layouts  1.32 us

profile of v2, /device:TPU:1, one launch (start us, length us, event | category | flops | bytes accessed | tf_op | source)
XLA Modules:
  0.0 42.0 jit_solution(2793199987722395017)
XLA Ops:
  0.0 40.7 %shard_map.55 = f32[4,8,128]{2,1,0:T(8,128)} custom-call(f32[2048,128]{1,0:T(8,128)} %bitcast.4, bf16[2048,128]{1,0:T(8,128)(2,1)} %bitcast.5, f32[16,1024]{1,0:T(8,128)} %gain_hbm.1, s32[1,128]{1,0:T(1,128)} %bitcast.6, s32[1,128]{1,0:T(1,128)} %bitcast.7), custom_call_target="tpu_custom_call" | custom-call | tf_op jit(solution)/shard_map/pallas_call | solution.py:338
  40.7 1.3 %copy.7 = f32[4,8,128]{2,1,0:T(8,128)} copy(f32[4,8,128]{2,1,0:T(8,128)} %shard_map.55) | data formatting | bytes 32768

commit v3 on v2

--- a/solution.py
+++ b/solution.py
@@ -74,7 +74,7 @@
 def kernel(
     alpha_hbm, perturb_hbm, gain_hbm, bands_hbm, steps_hbm, out_ref,
     alpha_ref, perturb_ref, gain_ref, bands_ref, steps_ref,
-    whi, wlo, vext, sib, hsend, hrecv, ub0, ub1, cf, af, gt, pf, pt, psend, smo, xs, xr, acc, zs, zr,
+    whi, wlo, vext, sib, hsend, hrecv, ub0, ub1, cf, af, gt, pf, pt, psend, smo, xs, xq, xscale, xr, xrscale, acc, zs, zr,
     in_sem, hs_sem, hr_sem, ps_sem, pr_sem, xs_sem, xr_sem, zs_sem, zr_sem,
 ):
     h = lax.axis_index("lat")
@@ -167,24 +167,21 @@
 
     for cp in loads[2:6]:
         cp.wait()
+    lax.fori_loop(0, 4, vertical, 0)
+    pl.semaphore_wait(barrier, len(partners))
+    own_pairs = pl.ds(h * 4, 4)
+    sends = [
+        (hsend.at[0, 0], hrecv.at[1, own_pairs], (h, gl, mi)),
+        (hsend.at[0, 1], hrecv.at[0, own_pairs], (h, gr, mi)),
+        (hsend.at[1, 0], hrecv.at[1, own_pairs], (oh, gl, mi)),
+        (hsend.at[1, 1], hrecv.at[0, own_pairs], (oh, gr, mi)),
+        (sib, vext.at[pl.ds(h * 8, 8), pl.ds(HALO, TILE)], (oh, g, mi)),
+    ]
     halo_copies = []
-    for b in range(2):
-        lax.fori_loop(2 * b, 2 * b + 2, vertical, 0)
-        if b == 0:
-            pl.semaphore_wait(barrier, len(partners))
-        own_pairs = pl.ds(h * 4 + 2 * b, 2)
-        pairs = pl.ds(2 * b, 2)
-        sends = [
-            (hsend.at[0, 0, pairs], hrecv.at[1, own_pairs], (h, gl, mi)),
-            (hsend.at[0, 1, pairs], hrecv.at[0, own_pairs], (h, gr, mi)),
-            (hsend.at[1, 0, pairs], hrecv.at[1, own_pairs], (oh, gl, mi)),
-            (hsend.at[1, 1, pairs], hrecv.at[0, own_pairs], (oh, gr, mi)),
-            (sib.at[pl.ds(4 * b, 4)], vext.at[pl.ds(h * 8 + 4 * b, 4), pl.ds(HALO, TILE)], (oh, g, mi)),
-        ]
-        for i, (src, dst, dev) in enumerate(sends):
-            cp = remote(src, dst, hs_sem.at[b, i], hr_sem.at[b, i], dev)
-            cp.start()
-            halo_copies.append(cp)
+    for i, (src, dst, dev) in enumerate(sends):
+        cp = remote(src, dst, hs_sem.at[i], hr_sem.at[i], dev)
+        cp.start()
+        halo_copies.append(cp)
 
     def widen(i, carry):
         at = pl.ds(pl.multiple_of(i * 256, 256), 256)
@@ -275,7 +272,12 @@
             product = smo[k, HALO : HALO + TILE, :].T * pt[y].astype(F32)
             total = (product[0:64, :] + product[64:128, :]) * 0.125
             for xx in range(NX):
-                xs[xx, y] = total[xx * 16 : (xx + 1) * 16, :]
+                part = total[xx * 16 : (xx + 1) * 16, :]
+                xs[xx, y] = part
+                peak = jnp.max(jnp.abs(part), axis=0, keepdims=True)
+                inverse = jnp.where(peak > 1e-30, 32767.0 / jnp.maximum(peak, 1e-30), 0.0)
+                xq[xx, y] = jnp.round(part * inverse).astype(jnp.int32).astype(jnp.int16)
+                xscale[xx, pl.ds(y, 1), :] = peak * (1.0 / 32767.0)
         return base
 
     xcopies = []
@@ -284,13 +286,20 @@
         lax.fori_loop(0, 2, weigh, base)
         half = pl.ds(base, 8)
         group = []
-        for d in range(1, NX):
-            cp = remote(
-                xs.at[lax.rem(x + d, NX), half], xr.at[d - 1, half],
-                xs_sem.at[e, d - 1], xr_sem.at[e, d - 1], (h, g, xmem(d)),
-            )
-            cp.start()
-            group.append(cp)
+        for d in (2, 1, 3):
+            to = lax.rem(x + d, NX)
+            for cp in (
+                remote(
+                    xq.at[to, half], xr.at[d - 1, half],
+                    xs_sem.at[e, d - 1, 0], xr_sem.at[e, d - 1, 0], (h, g, xmem(d)),
+                ),
+                remote(
+                    xscale.at[to, half], xrscale.at[d - 1, half],
+                    xs_sem.at[e, d - 1, 1], xr_sem.at[e, d - 1, 1], (h, g, xmem(d)),
+                ),
+            ):
+                cp.start()
+                group.append(cp)
         xcopies.append(group)
 
     zcopies = []
@@ -302,14 +311,17 @@
 
         def gather(i, carry):
             y = base + i
-            acc[pl.ds(pl.multiple_of(y * 16, 16), 16), :] = (xs[x, y] + xr[0, y]) + (xr[1, y] + xr[2, y])
+            total = xs[x, y]
+            for d in range(NX - 1):
+                total = total + xr[d, y].astype(jnp.int32).astype(F32) * xrscale[d, pl.ds(y, 1), :]
+            acc[pl.ds(pl.multiple_of(y * 16, 16), 16), :] = total
             return carry
 
         lax.fori_loop(0, 8, gather, 0)
         for zz in range(NZ):
             for lv in range(2):
                 zs[zz, e, lv] = acc[pl.ds(to * 128 + lv * 8 + zz, 8, stride=16), :]
-        for d in range(NZ):
+        for d in (4, 3, 5, 2, 6, 1, 7, 0):
             if d == 0 and e == 0:
                 continue
             cp = remote(
@@ -362,12 +374,15 @@
             pltpu.VMEM((8, 128, TILE), BF16),
             pltpu.VMEM((4, EXT, 128), F32),
             pltpu.VMEM((NX, ROWS, 16, TILE), F32),
-            pltpu.VMEM((NX - 1, ROWS, 16, TILE), F32),
+            pltpu.VMEM((NX, ROWS, 16, TILE), jnp.int16),
+            pltpu.VMEM((NX, ROWS, TILE), F32),
+            pltpu.VMEM((NX - 1, ROWS, 16, TILE), jnp.int16),
+            pltpu.VMEM((NX - 1, ROWS, TILE), F32),
             pltpu.VMEM((256, TILE), F32),
             pltpu.VMEM((NZ, 2, 2, 8, TILE), F32),
             pltpu.VMEM((2 * NZ, 2, 8, TILE), F32),
-            dma((8,)), dma((2, 5)), dma((2, 5)), dma((1,)), dma((1,)),
-            dma((2, 3)), dma((2, 3)), dma((16,)), dma((16,)),
+            dma((8,)), dma((5,)), dma((5,)), dma((1,)), dma((1,)),
+            dma((2, 3, 2)), dma((2, 3, 2)), dma((16,)), dma((16,)),
         ],
         compiler_params=pltpu.CompilerParams(
             collective_id=0, has_side_effects=True, vmem_limit_bytes=60 << 20

time: 42.2 us -> 40.1 us (0.950)
  Pallas kernels: 40.7 us -> 38.6 us
    pallas_call x1, Pallas kernels: 40.7 us -> 38.6 us  [body(): pl.pallas_call(kernel, out_shape=jax.ShapeDtypeStruct((4, 8, TILE), F32),...]
where the time goes in v3:
time: 40.1 us; the launch traced here: 39.9 us
  Pallas kernels  38.6 us (96%)
  local copies, waits for them, and re-layouts  1.32 us (3%)
    pallas_call x1, Pallas kernels, body(): pl.pallas_call(kernel, out_shape=jax.ShapeDtypeStruct((4, 8, TILE), F32),...  38.6 us
    unnamed x1, local copies, waits for them, and re-layouts  1.32 us

profile of v3, /device:TPU:1, one launch (start us, length us, event | category | flops | bytes accessed | tf_op | source)
XLA Modules:
  0.0 39.9 jit_solution(9141457553262886708)
XLA Ops:
  0.0 38.6 %shard_map.55 = f32[4,8,128]{2,1,0:T(8,128)} custom-call(f32[2048,128]{1,0:T(8,128)} %bitcast.4, bf16[2048,128]{1,0:T(8,128)(2,1)} %bitcast.5, f32[16,1024]{1,0:T(8,128)} %gain_hbm.1, s32[1,128]{1,0:T(1,128)} %bitcast.6, s32[1,128]{1,0:T(1,128)} %bitcast.7), custom_call_target="tpu_custom_call" | custom-call | tf_op jit(solution)/shard_map/pallas_call | solution.py:350
  38.6 1.3 %copy.7 = f32[4,8,128]{2,1,0:T(8,128)} copy(f32[4,8,128]{2,1,0:T(8,128)} %shard_map.55) | data formatting | bytes 32768

commit v4 on v3

--- a/solution.py
+++ b/solution.py
@@ -75,7 +75,7 @@
     alpha_hbm, perturb_hbm, gain_hbm, bands_hbm, steps_hbm, out_ref,
     alpha_ref, perturb_ref, gain_ref, bands_ref, steps_ref,
     whi, wlo, vext, sib, hsend, hrecv, ub0, ub1, cf, af, gt, pf, pt, psend, smo, xs, xq, xscale, xr, xrscale, acc, zs, zr,
-    in_sem, hs_sem, hr_sem, ps_sem, pr_sem, xs_sem, xr_sem, zs_sem, zr_sem,
+    in_sem, relay, hs_sem, hr_sem, ps_sem, pr_sem, xs_sem, xr_sem, zs_sem, zr_sem,
 ):
     h = lax.axis_index("lat")
     g = lax.axis_index("lon")
@@ -94,8 +94,8 @@
 
     partners = [(oh, g, mi)]
     partners += [(a, b, mi) for a in (h, oh) for b in (gl, gr)]
-    partners += [(h, g, xmem(d)) for d in range(1, NX)]
-    partners += [(a, g, zmem(d)) for a in (h, oh) for d in range(1, NZ)]
+    ring = [(h, g, zmem(1)), (h, g, zmem(NZ - 1)), (h, g, xmem(1)), (h, g, xmem(NX - 1))]
+    partners += ring
     barrier = pltpu.get_barrier_semaphore()
     for p in partners:
         pl.semaphore_signal(barrier, inc=1, device_id=p, device_id_type=pl.DeviceIdType.MESH)
@@ -111,6 +111,16 @@
     loads.append(pltpu.make_async_copy(perturb_hbm, perturb_ref, in_sem.at[7]))
     for cp in loads:
         cp.start()
+
+    def relay_send(r):
+        for i in range(4 if r == 1 else 2):
+            pl.semaphore_signal(
+                relay.at[r - 1, i], inc=1, device_id=ring[i], device_id_type=pl.DeviceIdType.MESH
+            )
+
+    def relay_wait(r):
+        for i in range(4 if r == 1 else 2):
+            pl.semaphore_wait(relay.at[r - 1, i], 1)
 
     def remote(src, dst, ssem, rsem, dev):
         return pltpu.make_async_remote_copy(
@@ -167,21 +177,25 @@
 
     for cp in loads[2:6]:
         cp.wait()
-    lax.fori_loop(0, 4, vertical, 0)
-    pl.semaphore_wait(barrier, len(partners))
-    own_pairs = pl.ds(h * 4, 4)
-    sends = [
-        (hsend.at[0, 0], hrecv.at[1, own_pairs], (h, gl, mi)),
-        (hsend.at[0, 1], hrecv.at[0, own_pairs], (h, gr, mi)),
-        (hsend.at[1, 0], hrecv.at[1, own_pairs], (oh, gl, mi)),
-        (hsend.at[1, 1], hrecv.at[0, own_pairs], (oh, gr, mi)),
-        (sib, vext.at[pl.ds(h * 8, 8), pl.ds(HALO, TILE)], (oh, g, mi)),
-    ]
     halo_copies = []
-    for i, (src, dst, dev) in enumerate(sends):
-        cp = remote(src, dst, hs_sem.at[i], hr_sem.at[i], dev)
-        cp.start()
-        halo_copies.append(cp)
+    for b in range(2):
+        lax.fori_loop(2 * b, 2 * b + 2, vertical, 0)
+        if b == 0:
+            pl.semaphore_wait(barrier, len(partners))
+            relay_send(1)
+        own_pairs = pl.ds(h * 4 + 2 * b, 2)
+        pairs = pl.ds(2 * b, 2)
+        sends = [
+            (hsend.at[0, 0, pairs], hrecv.at[1, own_pairs], (h, gl, mi)),
+            (hsend.at[0, 1, pairs], hrecv.at[0, own_pairs], (h, gr, mi)),
+            (hsend.at[1, 0, pairs], hrecv.at[1, own_pairs], (oh, gl, mi)),
+            (hsend.at[1, 1, pairs], hrecv.at[0, own_pairs], (oh, gr, mi)),
+            (sib.at[pl.ds(4 * b, 4)], vext.at[pl.ds(h * 8 + 4 * b, 4), pl.ds(HALO, TILE)], (oh, g, mi)),
+        ]
+        for i, (src, dst, dev) in enumerate(sends):
+            cp = remote(src, dst, hs_sem.at[b, i], hr_sem.at[b, i], dev)
+            cp.start()
+            halo_copies.append(cp)
 
     def widen(i, carry):
         at = pl.ds(pl.multiple_of(i * 256, 256), 256)
@@ -221,17 +235,21 @@
     gt[HALO : HALO + TILE, :] = gain_tile(g)
     gt[HALO + TILE :, :] = gain_tile(gr)[:HALO, :]
 
-    def spread(j, carry):
-        columns = gt[pl.ds(j, 8, stride=NJ), :]
-        at = pl.ds(pl.multiple_of(j * 8, 8), 8)
-        for y in range(ROWS):
-            c = jnp.broadcast_to(columns[:, y : y + 1], (8, 128))
-            cf[y, at, :] = c
-            af[y, at, :] = 1.0 - 4.0 * c
-        return carry
-
-    lax.fori_loop(0, NJ, spread, 0)
-
+    def spread(i, carry):
+        for k in range(2):
+            j = 2 * i + k
+            columns = gt[pl.ds(j, 8, stride=NJ), :]
+            at = pl.ds(pl.multiple_of(j * 8, 8), 8)
+            for y in range(ROWS):
+                c = jnp.broadcast_to(columns[:, y : y + 1], (8, 128))
+                cf[y, at, :] = c
+                af[y, at, :] = 1.0 - 4.0 * c
+        return carry
+
+    lax.fori_loop(0, NJ // 2, spread, 0)
+
+    relay_wait(1)
+    relay_send(2)
     for cp in halo_copies:
         cp.wait_recv()
 
@@ -248,6 +266,8 @@
 
     lax.fori_loop(0, ROWS // 2, restride, 0)
 
+    relay_wait(2)
+    relay_send(3)
     sub = iota((8, 128), 0)
     lclamp = jnp.logical_and(sub == HALO // NJ, g == 0)
     rclamp = jnp.logical_and(sub == (HALO + TILE - 1) // NJ, g == LON - 1)
@@ -258,7 +278,11 @@
         diffuse_step(ub1, ub0, cf, af, t + 1.0 < count, lclamp, rclamp, 8)
         return carry
 
-    lax.fori_loop(0, MAX_STEPS // 2, two_steps, 0)
+    lax.fori_loop(0, MAX_STEPS // 4, two_steps, 0)
+    relay_wait(3)
+    relay_send(4)
+    lax.fori_loop(MAX_STEPS // 4, MAX_STEPS // 2, two_steps, 0)
+    relay_wait(4)
 
     pcopy.wait_recv()
 
@@ -381,7 +405,7 @@
             pltpu.VMEM((256, TILE), F32),
             pltpu.VMEM((NZ, 2, 2, 8, TILE), F32),
             pltpu.VMEM((2 * NZ, 2, 8, TILE), F32),
-            dma((8,)), dma((5,)), dma((5,)), dma((1,)), dma((1,)),
+            dma((8,)), pltpu.SemaphoreType.REGULAR((4, 4)), dma((2, 5)), dma((2, 5)), dma((1,)), dma((1,)),
             dma((2, 3, 2)), dma((2, 3, 2)), dma((16,)), dma((16,)),
         ],
         compiler_params=pltpu.CompilerParams(

time: 40.1 us -> 39.3 us (0.980)
  Pallas kernels: 38.6 us -> 37.7 us
    pallas_call x1, Pallas kernels: 38.6 us -> 37.7 us  [body(): pl.pallas_call(kernel, out_shape=jax.ShapeDtypeStruct((4, 8, TILE), F32),...]
where the time goes in v4:
time: 39.3 us; the launch traced here: 39.1 us
  Pallas kernels  37.7 us (96%)
  local copies, waits for them, and re-layouts  1.32 us (3%)
    pallas_call x1, Pallas kernels, body(): pl.pallas_call(kernel, out_shape=jax.ShapeDtypeStruct((4, 8, TILE), F32),...  37.7 us
    unnamed x1, local copies, waits for them, and re-layouts  1.32 us

profile of v4, /device:TPU:1, one launch (start us, length us, event | category | flops | bytes accessed | tf_op | source)
XLA Modules:
  0.0 39.1 jit_solution(1407997951188292924)
XLA Ops:
  0.0 37.7 %shard_map.55 = f32[4,8,128]{2,1,0:T(8,128)} custom-call(f32[2048,128]{1,0:T(8,128)} %bitcast.4, bf16[2048,128]{1,0:T(8,128)(2,1)} %bitcast.5, f32[16,1024]{1,0:T(8,128)} %gain_hbm.1, s32[1,128]{1,0:T(1,128)} %bitcast.6, s32[1,128]{1,0:T(1,128)} %bitcast.7), custom_call_target="tpu_custom_call" | custom-call | tf_op jit(solution)/shard_map/pallas_call | solution.py:374
  37.8 1.3 %copy.7 = f32[4,8,128]{2,1,0:T(8,128)} copy(f32[4,8,128]{2,1,0:T(8,128)} %shard_map.55) | data formatting | bytes 32768

commit v5 on v4

--- a/solution.py
+++ b/solution.py
@@ -74,7 +74,7 @@
 def kernel(
     alpha_hbm, perturb_hbm, gain_hbm, bands_hbm, steps_hbm, out_ref,
     alpha_ref, perturb_ref, gain_ref, bands_ref, steps_ref,
-    whi, wlo, vext, sib, hsend, hrecv, ub0, ub1, cf, af, gt, pf, pt, psend, smo, xs, xq, xscale, xr, xrscale, acc, zs, zr,
+    whi, wlo, vext, sib, hsend, hrecv, ub0, ub1, cf, af, gt, pf, pt, psend, smo, xs, xq, xpeak, xr, xscale, acc, zs, zr,
     in_sem, relay, hs_sem, hr_sem, ps_sem, pr_sem, xs_sem, xr_sem, zs_sem, zr_sem,
 ):
     h = lax.axis_index("lat")
@@ -286,44 +286,43 @@
 
     pcopy.wait_recv()
 
-    def weigh(i, base):
-        for k in range(4):
-            y = base + 4 * i + k
-            for j in range(NJ):
-                smo[k, pl.ds(j, 8, stride=NJ), :] = ub0[y, j * 8 : (j + 1) * 8, :]
-        for k in range(4):
-            y = base + 4 * i + k
-            product = smo[k, HALO : HALO + TILE, :].T * pt[y].astype(F32)
-            total = (product[0:64, :] + product[64:128, :]) * 0.125
-            for xx in range(NX):
-                part = total[xx * 16 : (xx + 1) * 16, :]
-                xs[xx, y] = part
-                peak = jnp.max(jnp.abs(part), axis=0, keepdims=True)
-                inverse = jnp.where(peak > 1e-30, 32767.0 / jnp.maximum(peak, 1e-30), 0.0)
-                xq[xx, y] = jnp.round(part * inverse).astype(jnp.int32).astype(jnp.int16)
-                xscale[xx, pl.ds(y, 1), :] = peak * (1.0 / 32767.0)
-        return base
-
     xcopies = []
     for e in (1, 0):
         base = 8 * lax.rem(h + e, 2)
-        lax.fori_loop(0, 2, weigh, base)
-        half = pl.ds(base, 8)
+
+        def weigh(i, carry):
+            for k in range(4):
+                y = base + 4 * i + k
+                for j in range(NJ):
+                    smo[k, pl.ds(j, 8, stride=NJ), :] = ub0[y, j * 8 : (j + 1) * 8, :]
+            for k in range(4):
+                row = 4 * i + k
+                y = base + row
+                product = smo[k, HALO : HALO + TILE, :].T * pt[y].astype(F32)
+                total = (product[0:64, :] + product[64:128, :]) * 0.125
+                for xx in range(NX):
+                    part = total[xx * 16 : (xx + 1) * 16, :]
+                    xs[xx, y] = part
+                    xpeak[xx, pl.ds(row, 1), :] = jnp.max(jnp.abs(part), axis=0, keepdims=True)
+            return carry
+
+        lax.fori_loop(0, 2, weigh, 0)
         group = []
         for d in (2, 1, 3):
-            to = lax.rem(x + d, NX)
-            for cp in (
-                remote(
-                    xq.at[to, half], xr.at[d - 1, half],
-                    xs_sem.at[e, d - 1, 0], xr_sem.at[e, d - 1, 0], (h, g, xmem(d)),
-                ),
-                remote(
-                    xscale.at[to, half], xrscale.at[d - 1, half],
-                    xs_sem.at[e, d - 1, 1], xr_sem.at[e, d - 1, 1], (h, g, xmem(d)),
-                ),
-            ):
-                cp.start()
-                group.append(cp)
+            t = lax.rem(x + d, NX)
+            code = jnp.ceil(jnp.log2(jnp.maximum(xpeak[t], 1e-30)) * 256.0) + 1.0
+            inverse = 32700.0 / jnp.exp2(code * (1.0 / 256.0))
+            for row in range(8):
+                part = xs[t, base + row] * inverse[row : row + 1, :]
+                xq[d - 1, e, row] = jnp.round(part).astype(jnp.int32).astype(jnp.int16)
+            codes = jnp.concatenate([code, code], axis=0)
+            xq[d - 1, e, 8] = codes.astype(jnp.int32).astype(jnp.int16)
+            cp = remote(
+                xq.at[d - 1, e], xr.at[d - 1, e],
+                xs_sem.at[e, d - 1], xr_sem.at[e, d - 1], (h, g, xmem(d)),
+            )
+            cp.start()
+            group.append(cp)
         xcopies.append(group)
 
     zcopies = []
@@ -333,11 +332,15 @@
         for cp in group:
             cp.wait_recv()
 
+        for d in range(NX - 1):
+            codes = xr[d, e, 8].astype(jnp.int32).astype(F32)[0:8]
+            xscale[d] = jnp.exp2(codes * (1.0 / 256.0)) * (1.0 / 32700.0)
+
         def gather(i, carry):
             y = base + i
             total = xs[x, y]
             for d in range(NX - 1):
-                total = total + xr[d, y].astype(jnp.int32).astype(F32) * xrscale[d, pl.ds(y, 1), :]
+                total = total + xr[d, e, i].astype(jnp.int32).astype(F32) * xscale[d, pl.ds(i, 1), :]
             acc[pl.ds(pl.multiple_of(y * 16, 16), 16), :] = total
             return carry
 
@@ -398,15 +401,15 @@
             pltpu.VMEM((8, 128, TILE), BF16),
             pltpu.VMEM((4, EXT, 128), F32),
             pltpu.VMEM((NX, ROWS, 16, TILE), F32),
-            pltpu.VMEM((NX, ROWS, 16, TILE), jnp.int16),
-            pltpu.VMEM((NX, ROWS, TILE), F32),
-            pltpu.VMEM((NX - 1, ROWS, 16, TILE), jnp.int16),
-            pltpu.VMEM((NX - 1, ROWS, TILE), F32),
+            pltpu.VMEM((NX - 1, 2, 9, 16, TILE), jnp.int16),
+            pltpu.VMEM((NX, 8, TILE), F32),
+            pltpu.VMEM((NX - 1, 2, 9, 16, TILE), jnp.int16),
+            pltpu.VMEM((NX - 1, 8, TILE), F32),
             pltpu.VMEM((256, TILE), F32),
             pltpu.VMEM((NZ, 2, 2, 8, TILE), F32),
             pltpu.VMEM((2 * NZ, 2, 8, TILE), F32),
             dma((8,)), pltpu.SemaphoreType.REGULAR((4, 4)), dma((2, 5)), dma((2, 5)), dma((1,)), dma((1,)),
-            dma((2, 3, 2)), dma((2, 3, 2)), dma((16,)), dma((16,)),
+            dma((2, 3)), dma((2, 3)), dma((16,)), dma((16,)),
         ],
         compiler_params=pltpu.CompilerParams(
             collective_id=0, has_side_effects=True, vmem_limit_bytes=60 << 20

time: 39.3 us -> 39.1 us (level)
  no operation moved by 1% of the time
where the time goes in v5:
time: 39.1 us; the launch traced here: 38.9 us
  Pallas kernels  37.6 us (96%)
  local copies, waits for them, and re-layouts  1.32 us (3%)
    pallas_call x1, Pallas kernels, body(): pl.pallas_call(kernel, out_shape=jax.ShapeDtypeStruct((4, 8, TILE), F32),...  37.6 us
    unnamed x1, local copies, waits for them, and re-layouts  1.32 us

profile of v5, /device:TPU:1, one launch (start us, length us, event | category | flops | bytes accessed | tf_op | source)
XLA Modules:
  0.0 38.9 jit_solution(5590595049429561466)
XLA Ops:
  0.0 37.6 %shard_map.55 = f32[4,8,128]{2,1,0:T(8,128)} custom-call(f32[2048,128]{1,0:T(8,128)} %bitcast.4, bf16[2048,128]{1,0:T(8,128)(2,1)} %bitcast.5, f32[16,1024]{1,0:T(8,128)} %gain_hbm.1, s32[1,128]{1,0:T(1,128)} %bitcast.6, s32[1,128]{1,0:T(1,128)} %bitcast.7), custom_call_target="tpu_custom_call" | custom-call | tf_op jit(solution)/shard_map/pallas_call | solution.py:377
  37.6 1.3 %copy.7 = f32[4,8,128]{2,1,0:T(8,128)} copy(f32[4,8,128]{2,1,0:T(8,128)} %shard_map.55) | data formatting | bytes 32768

commit v6 on v5

--- a/solution.py
+++ b/solution.py
@@ -11,6 +11,7 @@
 TILE = 128
 EXT = TILE + 2 * HALO
 NJ = EXT // 8
+PAD = EXT + 24
 ROWS = 16
 MAX_STEPS = 24
 NX = 4
@@ -233,7 +234,7 @@
 
     gt[0:HALO, :] = gain_tile(gl)[TILE - HALO :, :]
     gt[HALO : HALO + TILE, :] = gain_tile(g)
-    gt[HALO + TILE :, :] = gain_tile(gr)[:HALO, :]
+    gt[HALO + TILE : EXT, :] = gain_tile(gr)[:HALO, :]
 
     def spread(i, carry):
         for k in range(2):
@@ -259,7 +260,7 @@
         for i in range(2):
             y = 2 * p + i
             vext[y, 0:HALO, :] = lefts[i * HALO : (i + 1) * HALO]
-            vext[y, HALO + TILE :, :] = rights[i * HALO : (i + 1) * HALO]
+            vext[y, HALO + TILE : EXT, :] = rights[i * HALO : (i + 1) * HALO]
             for j in range(NJ):
                 ub0[y, j * 8 : (j + 1) * 8, :] = vext[y, pl.ds(j, 8, stride=NJ), :]
         return carry
@@ -380,14 +381,14 @@
         in_specs=[pl.BlockSpec(memory_space=pl.ANY)] * 5,
         out_specs=vmem,
         scratch_shapes=[
-            pltpu.VMEM((2048, TILE), F32),
+            pltpu.VMEM((2048 + 16, TILE), F32),
             pltpu.VMEM((2048, TILE), BF16),
             pltpu.VMEM((ROWS, LON * TILE), F32),
             pltpu.VMEM((1, 128), jnp.int32),
             pltpu.VMEM((1, 128), jnp.int32),
             pltpu.VMEM((256, 256), BF16),
             pltpu.VMEM((256, 256), BF16),
-            pltpu.VMEM((ROWS, EXT, 128), F32),
+            pltpu.VMEM((ROWS, PAD, 128), F32),
             pltpu.VMEM((8, TILE, 128), F32),
             pltpu.VMEM((2, 2, 4, 2 * HALO, 128), BF16),
             pltpu.VMEM((2, ROWS // 2, 2 * HALO, 128), BF16),
@@ -395,17 +396,17 @@
             pltpu.VMEM((ROWS, EXT, 128), F32),
             pltpu.VMEM((ROWS, EXT, 128), F32),
             pltpu.VMEM((ROWS, EXT, 128), F32),
-            pltpu.VMEM((EXT, 128), F32),
-            pltpu.VMEM((2048, 128), F32),
+            pltpu.VMEM((PAD, 128), F32),
+            pltpu.VMEM((2048 + 256, 128), F32),
             pltpu.VMEM((ROWS, 128, TILE), BF16),
             pltpu.VMEM((8, 128, TILE), BF16),
-            pltpu.VMEM((4, EXT, 128), F32),
+            pltpu.VMEM((4, PAD, 128), F32),
             pltpu.VMEM((NX, ROWS, 16, TILE), F32),
             pltpu.VMEM((NX - 1, 2, 9, 16, TILE), jnp.int16),
             pltpu.VMEM((NX, 8, TILE), F32),
             pltpu.VMEM((NX - 1, 2, 9, 16, TILE), jnp.int16),
             pltpu.VMEM((NX - 1, 8, TILE), F32),
-            pltpu.VMEM((256, TILE), F32),
+            pltpu.VMEM((256 + 16, TILE), F32),
             pltpu.VMEM((NZ, 2, 2, 8, TILE), F32),
             pltpu.VMEM((2 * NZ, 2, 8, TILE), F32),
             dma((8,)), pltpu.SemaphoreType.REGULAR((4, 4)), dma((2, 5)), dma((2, 5)), dma((1,)), dma((1,)),

time: 39.1 us -> 39.1 us (level)
  no operation moved by 1% of the time
where the time goes in v6:
time: 39.1 us; the launch traced here: 39 us
  Pallas kernels  37.6 us (96%)
  local copies, waits for them, and re-layouts  1.32 us (3%)
    pallas_call x1, Pallas kernels, body(): pl.pallas_call(kernel, out_shape=jax.ShapeDtypeStruct((4, 8, TILE), F32),...  37.6 us
    unnamed x1, local copies, waits for them, and re-layouts  1.32 us

profile of v6, /device:TPU:1, one launch (start us, length us, event | category | flops | bytes accessed | tf_op | source)
XLA Modules:
  0.0 39.0 jit_solution(12156120869547207251)
XLA Ops:
  0.0 37.6 %shard_map.55 = f32[4,8,128]{2,1,0:T(8,128)} custom-call(f32[2048,128]{1,0:T(8,128)} %bitcast.4, bf16[2048,128]{1,0:T(8,128)(2,1)} %bitcast.5, f32[16,1024]{1,0:T(8,128)} %gain_hbm.1, s32[1,128]{1,0:T(1,128)} %bitcast.6, s32[1,128]{1,0:T(1,128)} %bitcast.7), custom_call_target="tpu_custom_call" | custom-call | tf_op jit(solution)/shard_map/pallas_call | solution.py:378
  37.6 1.3 %copy.7 = f32[4,8,128]{2,1,0:T(8,128)} copy(f32[4,8,128]{2,1,0:T(8,128)} %shard_map.55) | data formatting | bytes 32768
